TPU v7x, 32 devices: a whole 2x2x4 slice. The times are simulated.
32 devices in a mesh: grp: 2 (over y), row: 4 (over z), col: 2 (over x), sub: 2 (over core).
Axes of the slice: x: 2, y: 2, z: 4, core: 2. Of those that a mesh axis runs over, the one named last changes fastest.
Arguments:
- samples: bfloat16 [512, 2, 16, 512], P(('grp', 'row', 'col', 'sub')), parts along dimension 0, may hold values from -6 to 6
- analysis_taps: float32 [16, 16], replicated, may hold values from -1 to 1
- synthesis_taps: float32 [16, 16], replicated, may hold values from -1 to 1
- antenna_station: int32 [512], P('grp'), parts along dimension 0, may hold values from 0 to 31, as said below
- station_group: int32 [64, 1], P('grp'), parts along dimension 0, may hold values from 0 to 7
- beam_group: int32 [2048], P('grp'), parts along dimension 0, may hold values from 0 to 7
- beam_weights: bfloat16 [32, 2, 1024, 32], P(('grp', 'row'), None, ('col', 'sub')), parts along dimension 0, may hold values from -6 to 6
Outputs:
- visibilities: float32 [16, 2, 64, 32], P('row', None, ('grp', 'col', 'sub')), parts along dimension 2
- beam_series: float32 [2048, 2, 16, 512], P(('grp', 'col', 'sub', 'row')), parts along dimension 0
There are 2 independent parts, one for each index of `grp`. A program takes and returns all parts, laid end to end along the dimension named above; an argument that names none is the same for every part. Nothing has to cross between parts.
Inputs may be any that keep to these rules, and one draw needn't show every extreme that they name: `antenna_station`: every station is named by exactly 8 antennas.
All inputs are finite; a program needn't handle non-finite values.
Results may differ from a plain program's by a relative error of at most 0.005.
Values may be sent and summed in bfloat16 or wider, within the bound.
A program may use at most 64 MiB of HBM per device.

v0:
```python
import math
import jax
import jax.numpy as jnp
from jax import lax
from jax.sharding import PartitionSpec as P

ANTENNAS_PER_STN = 8
SPEC = 512


def polyphase(signal, coefficients):
    length = signal.shape[-1]
    output = coefficients[0][:, None] * signal
    for tap_index in range(1, coefficients.shape[0]):
        shifted = jnp.pad(
            signal[..., : length - tap_index], [(0, 0)] * (signal.ndim - 1) + [(tap_index, 0)]
        )
        output = output + coefficients[tap_index][:, None] * shifted
    return output


def fourier_table(length, direction):
    indices = jnp.arange(length)
    angles = (
        2.0 * math.pi / length * (indices[:, None] * indices[None, :] % length).astype(jnp.float32)
    )
    cosine_part = jnp.cos(angles)
    sine_part = jnp.sin(angles)
    table = jnp.stack(
        [
            jnp.stack([cosine_part, direction * sine_part]),
            jnp.stack([-direction * sine_part, cosine_part]),
        ]
    )
    return table.transpose(0, 2, 1, 3) * (1.0 / math.sqrt(length))


def body(
    samples, analysis_taps, synthesis_taps, antenna_station, station_group, beam_group, beam_weights
):
    high = lax.Precision.HIGHEST
    block_count = lax.axis_size(("col", "sub"))
    block_index = lax.axis_index(("col", "sub"))
    filtered = polyphase(samples.astype(jnp.float32), analysis_taps)
    spectra = jnp.einsum(
        "aqcf,qcpk->apkf", filtered, fourier_table(samples.shape[2], -1.0), precision=high
    ).astype(jnp.bfloat16)
    turned = lax.all_to_all(spectra, "row", split_axis=2, concat_axis=0, tiled=True)
    local_count = spectra.shape[0]
    held_rows = turned.shape[0]
    chan_rows = turned.shape[2]
    spec_len = turned.shape[3]
    station_count = station_group.shape[0]
    flat_width = 2 * chan_rows * spec_len
    tile_rows = station_count // block_count
    shard_rows = lax.all_gather(turned, ("col", "sub"), axis=0, tiled=True)
    row_total = shard_rows.shape[0]
    positions = jnp.arange(row_total, dtype=jnp.int32)
    source_block = positions // held_rows
    offset_rows = positions % held_rows
    source_row = offset_rows // local_count
    antenna = offset_rows % local_count
    global_index = (source_row * block_count + source_block) * local_count + antenna
    targets = antenna_station[global_index]
    wanted = jnp.arange(station_count, dtype=jnp.int32)
    one_hot = (targets[None, :] == wanted[:, None]).astype(jnp.bfloat16)
    summed_values = jnp.dot(
        one_hot, shard_rows.reshape(row_total, flat_width), preferred_element_type=jnp.float32
    )
    flat_stations = (summed_values * (1.0 / math.sqrt(ANTENNAS_PER_STN))).astype(jnp.bfloat16)
    station_list = flat_stations.reshape(station_count, 2, chan_rows, spec_len)
    real_part = station_list[:, 0]
    imag_part = station_list[:, 1]
    own_rows = lax.dynamic_slice_in_dim(station_list, block_index * tile_rows, tile_rows, 0)
    own_real = own_rows[:, 0]
    own_imag = own_rows[:, 1]
    vis_real = (
        jnp.einsum("icf,jcf->cij", own_real, real_part, preferred_element_type=jnp.float32)
        + jnp.einsum("icf,jcf->cij", own_imag, imag_part, preferred_element_type=jnp.float32)
    ) * (1.0 / SPEC)
    vis_imag = (
        jnp.einsum("icf,jcf->cij", own_imag, real_part, preferred_element_type=jnp.float32)
        - jnp.einsum("icf,jcf->cij", own_real, imag_part, preferred_element_type=jnp.float32)
    ) * (1.0 / SPEC)
    visibilities = jnp.stack([vis_real, vis_imag], axis=1)
    beam_block = beam_weights.shape[2]
    own_groups = lax.dynamic_slice_in_dim(beam_group, block_index * beam_block, beam_block, 0)
    members = station_group[:, 0][None, :] == own_groups[:, None]
    scaling = 1.0 / jnp.sqrt(jnp.sum(members.astype(jnp.float32), axis=1))
    weights = jnp.where(members[None, None], beam_weights, jnp.zeros((), jnp.bfloat16))
    weight_real = weights[:, 0]
    imaginary_weight = weights[:, 1]
    beam_real = jnp.einsum(
        "cbs,scf->bcf", weight_real, real_part, preferred_element_type=jnp.float32
    ) - jnp.einsum("cbs,scf->bcf", imaginary_weight, imag_part, preferred_element_type=jnp.float32)
    beam_imag = jnp.einsum(
        "cbs,scf->bcf", weight_real, imag_part, preferred_element_type=jnp.float32
    ) + jnp.einsum("cbs,scf->bcf", imaginary_weight, real_part, preferred_element_type=jnp.float32)
    beams = (jnp.stack([beam_real, beam_imag], axis=1) * scaling[:, None, None, None]).astype(
        jnp.bfloat16
    )
    returned = lax.all_to_all(beams, "row", split_axis=0, concat_axis=2, tiled=True)
    inverse = jnp.einsum(
        "bqkf,qkpc->bpcf",
        returned.astype(jnp.float32),
        fourier_table(returned.shape[2], 1.0),
        precision=high,
    )
    beam_series = polyphase(inverse, synthesis_taps)
    return (visibilities, beam_series)


def solution(mesh):
    return jax.shard_map(
        body,
        mesh=mesh,
        in_specs=(
            P(("grp", "row", "col", "sub"), None, None, None),
            P(),
            P(),
            P("grp"),
            P("grp", None),
            P("grp"),
            P(("grp", "row"), None, ("col", "sub"), None),
        ),
        out_specs=(
            P("row", None, ("grp", "col", "sub"), None),
            P(("grp", "col", "sub", "row"), None, None, None),
        ),
        check_vma=False,
    )
```

profile of v0, /device:TPU:0, one launch (start us, length us, event | category | flops | bytes accessed | tf_op | source)
XLA Modules:
  0.0 157.8 jit_solution(14489460331540854039)
XLA Ops:
  7.4 1.2 slice.274
  8.5 1.2 slice.275
  9.7 0.1 slice.276
  9.8 0.1 slice.277
  10.0 0.1 slice.278
  10.1 0.1 slice.279
  10.2 0.1 slice.280
  10.4 0.1 slice.281
  10.5 0.1 slice.282
  10.6 0.1 slice.283
  10.8 0.1 slice.284
  10.9 0.1 slice.285
  11.0 0.1 slice.286
  11.2 0.1 slice.287
  11.3 0.1 slice.288
  11.4 0.2 copy-done.3
  11.6 5.1 %fusion.3 = bf16[16,2,16,512]{3,2,0,1:T(8,128)(2,1)S(1)} fusion(f32[16,2,16,497]{3,2,1,0:T(8,128)S(1)} %slice.288, f32[16,2,16,498]{3,2,1,0:T(8,128)S(1)} %slice.287, f32[16,2,16,499]{3,2,1,0:T(8,128)S(1)} %slice.286, f32[16,2,16,500]{3,2,1,0:T(8,128)S(1)} %slice.285, f32[16,2,16,501]{3,2,1,0:T(8,128)S(1)} %slice.284, f32[16,2,16,502]{3,2,1,0:T(8,128)S(1)} %slice.283, ...), kind=kOutput, calls=%fused_computation.11 | convolution fusion | flops 109316096 | bytes 16536576 | tf_op jit(solution)/shard_map/aqcf,qcpk->apkf/dot_general | solution.py:45
  16.8 0.3 copy.55
  17.1 20.6 %all_to_all.36 = bf16[16,2,16,512]{3,0,1,2:T(8,128)(2,1)S(1)} all-to-all(bf16[16,2,16,512]{3,0,1,2:T(8,128)(2,1)S(1)} %copy.55), channel_id=1, replica_groups=mesh['grp'=2,'row'=4,'col'=2,'sub'=2] {'row'}, dimensions={2} | all-to-all | bytes 1048576 | tf_op jit(solution)/shard_map/all_to_all | solution.py:48
  37.7 0.8 copy.57
  38.5 0.8 dynamic_slice.7
  39.3 0.1 convert_reduce_fusion
  39.4 1.9 %gather_fusion = s32[256]{0:T(256)S(1)} fusion(s32[256]{0:T(256)S(1)} %copy-done, s32[1024]{0:T(1024)S(1)} %pad_clamp_fusion), kind=kCustom, calls=%fused_computation | custom fusion | bytes 3072 | tf_op jit(solution)/shard_map/gather | solution.py:64
  41.4 0.1 broadcast_compare_fusion
  41.5 18.9 %all-gather.2.cloned.1.call-done = bf16[256,2,4,512]{3,0,2,1:T(8,128)(2,1)} async-done(((bf16[64,2,4,512]{3,0,2,1:T(8,128)(2,1)}), bf16[256,2,4,512]{3,0,2,1:T(8,128)(2,1)}) %all-gather.2.cloned.1.call-update) | async-done | bytes 2097168 | tf_op jit(solution)/shard_map/all_gather | solution.py:56
  60.4 2.8 %copy.58 = bf16[256,2,4,512]{0,3,2,1:T(8,128)(2,1)S(1)} copy(bf16[256,2,4,512]{3,0,2,1:T(8,128)(2,1)} %all-gather.2.cloned.1.call-done) | data formatting | bytes 4194304 | tf_op jit(solution)/shard_map/all_gather | solution.py:56
  63.2 0.7 fusion
  63.9 0.2 reshape.289
  64.1 0.1 fusion.103
  64.2 0.5 fusion.72
  64.6 0.5 fusion.75
  65.1 0.5 subtract_bitcast_fusion
  65.6 0.5 add_bitcast_fusion
  66.1 0.4 fusion.1
  66.6 3.1 %copy.64 = bf16[256,2,4,512]{3,2,1,0:T(4,128)(2,1)} copy(bf16[256,2,4,512]{0,3,2,1:T(8,128)(2,1)S(1)} %fusion.1) | data formatting | bytes 4194304 | tf_op jit(solution)/shard_map/convert_element_type | solution.py:99
  69.6 4.6 %all-to-all-start.1 = ((bf16[256,2,4,512]{3,2,1,0:T(4,128)(2,1)}), bf16[256,2,4,512]{3,2,1,0:T(4,128)(2,1)S(1)}, u32[]{:S(2)}, u32[]{:S(2)}) async-start(bf16[256,2,4,512]{3,2,1,0:T(4,128)(2,1)} %copy.64), calls=%async_computation.1 | async-start | bytes 4194304 | tf_op jit(solution)/shard_map/all_to_all | solution.py:102
  74.3 0.1 fusion.74
  74.5 0.2 fusion.7
  74.6 0.1 fusion.73
  74.8 0.2 fusion.5
  74.9 0.6 copy.67
  75.6 47.3 %all-to-all-done.1 = bf16[256,2,4,512]{3,2,1,0:T(4,128)(2,1)S(1)} async-done(((bf16[256,2,4,512]{3,2,1,0:T(4,128)(2,1)}), bf16[256,2,4,512]{3,2,1,0:T(4,128)(2,1)S(1)}, u32[]{:S(2)}, u32[]{:S(2)}) %all-to-all-start.1) | async-done | bytes 2097184 | tf_op jit(solution)/shard_map/all_to_all | solution.py:102
  122.8 0.7 copy.65
  123.5 2.9 %copy.66 = bf16[64,2,4,4,512]{4,3,2,1,0:T(4,128)(2,1)} copy(bf16[64,2,4,4,512]{4,0,2,3,1:T(8,128)(2,1)S(1)} %bitcast.188) | data formatting | bytes 4194304 | tf_op jit(solution)/shard_map/all_to_all | solution.py:102
  126.5 2.5 %reshape.302 = bf16[64,2,16,512,1]{3,2,1,0,4:T(8,128)(2,1)S(1)} reshape(bf16[64,2,4,4,512]{4,3,2,1,0:T(4,128)(2,1)} %copy.66) | data formatting | bytes 4194304 | tf_op jit(solution)/shard_map/all_to_all | solution.py:102
  129.0 2.0 %convolution_bitcast_fusion = f32[64,2,16,512]{3,2,0,1:T(8,128)S(1)} fusion(bf16[64,2,16,512,1]{3,2,1,0,4:T(8,128)(2,1)S(1)} %reshape.302, f32[1,2,16,16]{2,3,0,1:T(8,128)S(1)} %get-tuple-element.37, f32[1,2,16,16]{2,3,0,1:T(8,128)S(1)} %get-tuple-element.16), kind=kOutput, calls=%fused_computation.6 | convolution fusion | flops 402655232 | bytes 6295552 | tf_op jit(solution)/shard_map/bqkf,qkpc->bpcf/dot_general | solution.py:103
  131.0 17.3 %multiply_add_fusion = f32[64,2,16,512]{3,2,0,1:T(8,128)S(1)} fusion(f32[64,2,16,497]{3,2,0,1:T(8,128)S(1)} %bitcast.172, f32[64,2,16,498]{3,2,0,1:T(8,128)S(1)} %bitcast.173, f32[64,2,16,499]{3,2,0,1:T(8,128)S(1)} %bitcast.174, f32[64,2,16,500]{3,2,0,1:T(8,128)S(1)} %bitcast.175, f32[64,2,16,501]{3,2,0,1:T(8,128)S(1)} %bitcast.176, ...), kind=kLoop, calls=%fused_computation.5 | loop fusion | flops 32505856 | bytes 70321152 | tf_op jit(solution)/shard_map/add | solution.py:18
  148.4 2.6 %copy.68 = f32[64,2,16,512]{3,2,1,0:T(8,128)} copy(f32[64,2,16,512]{3,2,0,1:T(8,128)S(1)} %multiply_add_fusion) | data formatting | bytes 8388608
  (24 shorter events, 0.3 us)
Async XLA Ops:
  7.2 32.3 %copy-start = (s32[256]{0:T(256)S(1)}, s32[256]{0:T(256)}, u32[]{:S(2)}) copy-start(s32[256]{0:T(256)} %param.10) | copy-start | bytes 3076
  7.2 2.5 %copy-start.1 = (bf16[16,2,16,512]{3,2,1,0:T(8,128)(2,1)S(1)}, bf16[16,2,16,512]{3,2,1,0:T(8,128)(2,1)}, u32[]{:S(2)}) copy-start(bf16[16,2,16,512]{3,2,1,0:T(8,128)(2,1)} %param.7) | copy-start | bytes 1572868
  7.2 53.2 %all-gather.2.cloned.1.call-start = ((), (), s32[]{:S(2)}) async-start(), calls=%async_computation.2 | async-start | bytes 2621440 | tf_op jit(solution)/shard_map/all_gather | solution.py:56
  10.9 0.7 copy-start.3
  11.6 27.7 %copy-start.5 = (s32[32,1]{0,1:T(1,128)S(1)}, s32[32,1]{0,1:T(1,128)}, u32[]{:S(2)}) copy-start(s32[32,1]{0,1:T(1,128)} %param.11) | copy-start | bytes 388
  16.7 24.7 %copy-start.2 = (bf16[4,2,256,32]{2,3,1,0:T(8,128)(2,1)S(1)}, bf16[4,2,256,32]{2,3,1,0:T(8,128)(2,1)}, u32[]{:S(2)}) copy-start(bf16[4,2,256,32]{2,3,1,0:T(8,128)(2,1)} %param.13) | copy-start | bytes 393220
  66.5 7.7 %copy-start.4 = (f32[16,16]{1,0:T(8,128)S(1)}, f32[16,16]{1,0:T(8,128)}, u32[]{:S(2)}) copy-start(f32[16,16]{1,0:T(8,128)} %param.9) | copy-start | bytes 3076
  69.6 53.2 %all-to-all-start.1 = ((bf16[256,2,4,512]{3,2,1,0:T(4,128)(2,1)}), bf16[256,2,4,512]{3,2,1,0:T(4,128)(2,1)S(1)}, u32[]{:S(2)}, u32[]{:S(2)}) async-start(bf16[256,2,4,512]{3,2,1,0:T(4,128)(2,1)} %copy.64), calls=%async_computation.1 | async-start | bytes 4194304 | tf_op jit(solution)/shard_map/all_to_all | solution.py:102
Sparse Core Ops, SparseCore 0:
  38.6 21.6 all-gather.1
where the time goes:
time: 158 us
  waiting for transfers between devices  66.2 us (42%)
  local copies, waits for them, and re-layouts  23.5 us (15%)
  blocking collectives  20.6 us (13%)
  other arithmetic  18.1 us (11%)
  between operations  14.4 us (9%)
  matrix products  10.3 us (7%)
  starting transfers between devices  4.66 us (3%)
    all_to_all x1, waiting for transfers between devices, body(): lax.all_to_all(beams, 'row', split_axis=0, concat_axis=2, tiled=True)  47.3 us
    all_to_all x1, blocking collectives, body(): lax.all_to_all(spectra, 'row', split_axis=2, concat_axis=0, tiled=True)  20.6 us
    all_gather x1, waiting for transfers between devices, body(): shard_rows = lax.all_gather(turned, ('col', 'sub'), axis=0, tiled=True)  18.9 us
    add x1, other arithmetic, polyphase(): output = output + coefficients[tap_index][:, None] * shifted  17.3 us
    all_to_all x3, local copies, waits for them, and re-layouts, body(): lax.all_to_all(beams, 'row', split_axis=0, concat_axis=2, tiled=True)  6.19 us
    dot_general x1, matrix products, body(): jnp.einsum('aqcf,qcpk->apkf', filtered, fourier_table(samples.shape[2], -...  5.12 us
    all_to_all x1, starting transfers between devices, body(): lax.all_to_all(beams, 'row', split_axis=0, concat_axis=2, tiled=True)  4.62 us
    slice x15, local copies, waits for them, and re-layouts, polyphase(): signal[..., :length - tap_index]  3.91 us
  transfers between devices with their start and end apart: 2, of which 2 were waited for; matrix products, arithmetic and copies ran while one was open for 3% of the time, Pallas kernels for 0%

commit v1 on v0

--- a/solution.py
+++ b/solution.py
@@ -6,6 +6,28 @@
 
 ANTENNAS_PER_STN = 8
 SPEC = 512
+
+
+def laid_out(tiles, dim):
+    shape = list(tiles.shape[1:])
+    shape[dim] *= tiles.shape[0]
+    return jnp.moveaxis(tiles, 0, dim).reshape(shape)
+
+
+def gather_around(value, axis, dim):
+    devices = lax.axis_size(axis)
+    pairs = [(i, (i + 1) % devices) for i in range(devices)]
+    back = [(b, a) for a, b in pairs]
+    lower, upper = ([], [])
+    for step in range(devices - 1):
+        if step % 2 == 0:
+            lower.append(lax.ppermute(lower[-1] if lower else value, axis, pairs))
+        else:
+            upper.append(lax.ppermute(upper[-1] if upper else value, axis, back))
+    blocks = jnp.stack([*lower[::-1], value, *upper])
+    shift = lax.axis_index(axis) - len(lower)
+    blocks = blocks[(jnp.arange(devices) - shift) % devices]
+    return laid_out(blocks, dim)
 
 
 def polyphase(signal, coefficients):
@@ -53,7 +75,7 @@
     station_count = station_group.shape[0]
     flat_width = 2 * chan_rows * spec_len
     tile_rows = station_count // block_count
-    shard_rows = lax.all_gather(turned, ("col", "sub"), axis=0, tiled=True)
+    shard_rows = gather_around(turned, ("col", "sub"), 0)
     row_total = shard_rows.shape[0]
     positions = jnp.arange(row_total, dtype=jnp.int32)
     source_block = positions // held_rows

time: 158 us -> 147 us (0.930)
  between operations: 14.4 us -> 1.04 us
  local copies, waits for them, and re-layouts: 23.5 us -> 29.8 us
  waiting for transfers between devices: 66.2 us -> 61.2 us
    all_gather x1 -> x0, waiting for transfers between devices: 18.9 us -> none  [body(): shard_rows = lax.all_gather(turned, ('col', 'sub'), axis=0, tiled=True)]
    ppermute x0 -> x3, waiting for transfers between devices: none -> 15 us  [the longest x2 10.6 us: gather_around(): lower.append(lax.ppermute(lower[-1] if lower else value, axis, pairs))]
    gather x0 -> x2, local copies, waits for them, and re-layouts: none -> 6.55 us  [gather_around(): blocks = blocks[(jnp.arange(devices) - shift) % devices]]
    another operation x0 -> x1, local copies, waits for them, and re-layouts: none -> 3.26 us  [body(): shard_rows.reshape(row_total, flat_width)]
    all_gather x1 -> x0, local copies, waits for them, and re-layouts: 2.77 us -> none  [body(): shard_rows = lax.all_gather(turned, ('col', 'sub'), axis=0, tiled=True)]
    ppermute x0 -> x3, starting transfers between devices: none -> 1.91 us  [the longest x1 1.77 us: gather_around(): upper.append(lax.ppermute(upper[-1] if upper else value, axis, back))]
  transfers between devices with their start and end apart: 2 -> 4, of which waited for: 2 -> 4; matrix products, arithmetic and copies ran while one was open for 3% -> 3% of each run, Pallas kernels for 0% -> 0%
where the time goes in v1:
time: 147 us
  waiting for transfers between devices  61.2 us (42%)
  local copies, waits for them, and re-layouts  29.8 us (20%)
  blocking collectives  20.6 us (14%)
  other arithmetic  18.4 us (13%)
  matrix products  10.1 us (7%)
  starting transfers between devices  5.74 us (4%)
    all_to_all x1, waiting for transfers between devices, body(): lax.all_to_all(beams, 'row', split_axis=0, concat_axis=2, tiled=True)  46.2 us
    all_to_all x1, blocking collectives, body(): lax.all_to_all(spectra, 'row', split_axis=2, concat_axis=0, tiled=True)  20.6 us
    add x1, other arithmetic, polyphase(): output = output + coefficients[tap_index][:, None] * shifted  17.3 us
    ppermute x2, waiting for transfers between devices, gather_around(): lower.append(lax.ppermute(lower[-1] if lower else value, axis, pairs))  10.6 us
    gather x2, local copies, waits for them, and re-layouts, gather_around(): blocks = blocks[(jnp.arange(devices) - shift) % devices]  6.55 us
    all_to_all x3, local copies, waits for them, and re-layouts, body(): lax.all_to_all(beams, 'row', split_axis=0, concat_axis=2, tiled=True)  6.19 us
    dot_general x1, matrix products, body(): jnp.einsum('aqcf,qcpk->apkf', filtered, fourier_table(samples.shape[2], -...  5.11 us
    ppermute x1, waiting for transfers between devices, gather_around(): upper.append(lax.ppermute(upper[-1] if upper else value, axis, back))  4.39 us
  transfers between devices with their start and end apart: 4, of which 4 were waited for; matrix products, arithmetic and copies ran while one was open for 3% of the time, Pallas kernels for 0%

profile of v1, /device:TPU:0, one launch (start us, length us, event | category | flops | bytes accessed | tf_op | source)
XLA Modules:
  0.0 146.8 jit_solution(10426498056328943073)
XLA Ops:
  0.8 1.2 slice.276
  2.0 1.2 slice.277
  3.3 0.1 slice.279
  3.4 0.1 slice.280
  3.6 0.1 slice.281
  3.7 0.1 slice.282
  3.8 0.1 slice.283
  4.0 0.1 slice.284
  4.1 0.1 slice.285
  4.2 0.1 slice.286
  4.5 0.1 slice.288
  4.7 0.1 slice.289
  4.8 0.1 slice.290
  4.9 0.2 copy-done.3
  5.1 5.1 %fusion.3 = bf16[16,2,16,512]{3,2,0,1:T(8,128)(2,1)S(1)} fusion(f32[16,2,16,497]{3,2,1,0:T(8,128)S(1)} %slice.290, f32[16,2,16,498]{3,2,1,0:T(8,128)S(1)} %slice.289, f32[16,2,16,499]{3,2,1,0:T(8,128)S(1)} %slice.288, f32[16,2,16,500]{3,2,1,0:T(8,128)S(1)} %slice.287, f32[16,2,16,501]{3,2,1,0:T(8,128)S(1)} %slice.286, f32[16,2,16,502]{3,2,1,0:T(8,128)S(1)} %slice.285, ...), kind=kOutput, calls=%fused_computation.13 | convolution fusion | flops 109316096 | bytes 16536576 | tf_op jit(solution)/shard_map/aqcf,qcpk->apkf/dot_general | solution.py:67
  10.2 0.3 copy.55
  10.5 20.6 %all_to_all.36 = bf16[16,2,16,512]{3,0,1,2:T(8,128)(2,1)S(1)} all-to-all(bf16[16,2,16,512]{3,0,1,2:T(8,128)(2,1)S(1)} %copy.55), channel_id=1, replica_groups=mesh['grp'=2,'row'=4,'col'=2,'sub'=2] {'row'}, dimensions={2} | all-to-all | bytes 1048576 | tf_op jit(solution)/shard_map/all_to_all | solution.py:70
  31.2 0.8 dynamic_slice.7
  32.2 1.9 %gather_fusion = s32[256]{0:T(256)S(1)} fusion(s32[256]{0:T(256)S(1)} %copy-done, s32[1024]{0:T(1024)S(1)} %pad_clamp_fusion.1), kind=kCustom, calls=%fused_computation | custom fusion | bytes 3072 | tf_op jit(solution)/shard_map/gather | solution.py:86
  34.1 1.8 %collective-permute-start.2 = (bf16[64,2,4,512]{3,0,2,1:T(8,128)(2,1)S(1)}, bf16[64,2,4,512]{3,0,2,1:T(8,128)(2,1)S(1)}, u32[]{:S(2)}, u32[]{:S(2)}) collective-permute-start(bf16[64,2,4,512]{3,0,2,1:T(8,128)(2,1)S(1)} %bitcast.197), channel_id=1, source_target_pairs={{1,0},{2,1},{3,2},{0,3},{5,4},{6,5},{7,6},{4,7},{9,8},{10,9},{11,1... | collective-permute-start | bytes 1572872 | tf_op jit(solution)/shard_map/ppermute | solution.py:26
  35.9 4.8 %collective-permute-done = bf16[64,2,4,512]{3,0,2,1:T(8,128)(2,1)S(1)} collective-permute-done((bf16[64,2,4,512]{3,0,2,1:T(8,128)(2,1)S(1)}, bf16[64,2,4,512]{3,0,2,1:T(8,128)(2,1)S(1)}, u32[]{:S(2)}, u32[]{:S(2)}) %collective-permute-start) | collective-permute-done | bytes 524320 | tf_op jit(solution)/shard_map/ppermute | solution.py:24
  40.9 4.4 %collective-permute-done.2 = bf16[64,2,4,512]{3,0,2,1:T(8,128)(2,1)S(1)} collective-permute-done((bf16[64,2,4,512]{3,0,2,1:T(8,128)(2,1)S(1)}, bf16[64,2,4,512]{3,0,2,1:T(8,128)(2,1)S(1)}, u32[]{:S(2)}, u32[]{:S(2)}) %collective-permute-start.2) | collective-permute-done | bytes 524320 | tf_op jit(solution)/shard_map/ppermute | solution.py:26
  45.2 5.8 %collective-permute-done.1 = bf16[64,2,4,512]{3,0,2,1:T(8,128)(2,1)S(1)} collective-permute-done((bf16[64,2,4,512]{3,0,2,1:T(8,128)(2,1)S(1)}, bf16[64,2,4,512]{3,0,2,1:T(8,128)(2,1)S(1)}, u32[]{:S(2)}, u32[]{:S(2)}) %collective-permute-start.1) | collective-permute-done | bytes 524320 | tf_op jit(solution)/shard_map/ppermute | solution.py:24
  51.1 0.3 pad_maximum_fusion
  51.3 2.0 %gather_fusion.1 = bf16[4,64,2,4,512]{4,1,3,2,0:T(8,128)(2,1)} fusion(bf16[4,64,2,4,512]{4,1,3,2,0:T(8,128)(2,1)S(1)} %pad_maximum_fusion, s32[1024]{0:T(1024)S(1)} %pad_clamp_fusion), kind=kCustom, calls=%fused_computation.1 | custom fusion | bytes 4194320 | tf_op jit(solution)/shard_map/gather | solution.py:29
  53.3 4.5 %copy.59 = bf16[4,64,2,4,512]{4,3,2,1,0:T(4,128)(2,1)} copy(bf16[4,64,2,4,512]{4,1,3,2,0:T(8,128)(2,1)} %gather_fusion.1) | data formatting | bytes 4194304 | tf_op jit(solution)/shard_map/gather | solution.py:29
  57.9 3.3 %reshape_reshape.3 = bf16[256,4096]{1,0:T(8,128)(2,1)S(1)} reshape(bf16[4,64,2,4,512]{4,3,2,1,0:T(4,128)(2,1)} %copy.59) | data formatting | bytes 4194304 | tf_op jit(solution)/shard_map/reshape;reshape | solution.py:90
  61.2 0.5 fusion
  61.6 0.2 reshape.335
  61.9 0.5 fusion.72
  62.4 0.5 fusion.75
  62.9 0.5 subtract_bitcast_fusion
  63.4 0.5 add_bitcast_fusion
  63.9 0.4 fusion.1
  64.3 3.1 %copy.65 = bf16[256,2,4,512]{3,2,1,0:T(4,128)(2,1)} copy(bf16[256,2,4,512]{0,3,2,1:T(8,128)(2,1)S(1)} %fusion.1) | data formatting | bytes 4194304 | tf_op jit(solution)/shard_map/convert_element_type | solution.py:121
  67.4 3.8 %all-to-all-start.1 = ((bf16[256,2,4,512]{3,2,1,0:T(4,128)(2,1)}), bf16[256,2,4,512]{3,2,1,0:T(4,128)(2,1)S(1)}, u32[]{:S(2)}, u32[]{:S(2)}) async-start(bf16[256,2,4,512]{3,2,1,0:T(4,128)(2,1)} %copy.65), calls=%async_computation.1 | async-start | bytes 4194304 | tf_op jit(solution)/shard_map/all_to_all | solution.py:124
  71.3 0.1 fusion.74
  71.4 0.2 fusion.7
  71.6 0.1 fusion.73
  71.8 0.2 fusion.5
  71.9 0.6 copy.68
  72.6 46.2 %all-to-all-done.1 = bf16[256,2,4,512]{3,2,1,0:T(4,128)(2,1)S(1)} async-done(((bf16[256,2,4,512]{3,2,1,0:T(4,128)(2,1)}), bf16[256,2,4,512]{3,2,1,0:T(4,128)(2,1)S(1)}, u32[]{:S(2)}, u32[]{:S(2)}) %all-to-all-start.1) | async-done | bytes 2097184 | tf_op jit(solution)/shard_map/all_to_all | solution.py:124
  118.7 0.7 copy.66
  119.4 2.9 %copy.67 = bf16[64,2,4,4,512]{4,3,2,1,0:T(4,128)(2,1)} copy(bf16[64,2,4,4,512]{4,0,2,3,1:T(8,128)(2,1)S(1)} %bitcast.194) | data formatting | bytes 4194304 | tf_op jit(solution)/shard_map/all_to_all | solution.py:124
  122.4 2.5 %reshape.356 = bf16[64,2,16,512,1]{3,2,1,0,4:T(8,128)(2,1)S(1)} reshape(bf16[64,2,4,4,512]{4,3,2,1,0:T(4,128)(2,1)} %copy.67) | data formatting | bytes 4194304 | tf_op jit(solution)/shard_map/all_to_all | solution.py:124
  124.9 2.0 %convolution_bitcast_fusion = f32[64,2,16,512]{3,2,0,1:T(8,128)S(1)} fusion(bf16[64,2,16,512,1]{3,2,1,0,4:T(8,128)(2,1)S(1)} %reshape.356, f32[1,2,16,16]{2,3,0,1:T(8,128)S(1)} %get-tuple-element.37, f32[1,2,16,16]{2,3,0,1:T(8,128)S(1)} %get-tuple-element.16), kind=kOutput, calls=%fused_computation.7 | convolution fusion | flops 402655232 | bytes 6295552 | tf_op jit(solution)/shard_map/bqkf,qkpc->bpcf/dot_general | solution.py:125
  126.9 17.3 %multiply_add_fusion = f32[64,2,16,512]{3,2,0,1:T(8,128)S(1)} fusion(f32[64,2,16,497]{3,2,0,1:T(8,128)S(1)} %bitcast.179, f32[64,2,16,498]{3,2,0,1:T(8,128)S(1)} %bitcast.180, f32[64,2,16,499]{3,2,0,1:T(8,128)S(1)} %bitcast.181, f32[64,2,16,500]{3,2,0,1:T(8,128)S(1)} %bitcast.182, f32[64,2,16,501]{3,2,0,1:T(8,128)S(1)} %bitcast.183, ...), kind=kLoop, calls=%fused_computation.6 | loop fusion | flops 32505856 | bytes 70321152 | tf_op jit(solution)/shard_map/add | solution.py:40
  144.3 2.6 %copy.69 = f32[64,2,16,512]{3,2,1,0:T(8,128)} copy(f32[64,2,16,512]{3,2,0,1:T(8,128)S(1)} %multiply_add_fusion) | data formatting | bytes 8388608
  (32 shorter events, 1.0 us)
Async XLA Ops:
  0.6 31.5 %copy-start = (s32[256]{0:T(256)S(1)}, s32[256]{0:T(256)}, u32[]{:S(2)}) copy-start(s32[256]{0:T(256)} %param.10) | copy-start | bytes 3076
  0.6 2.5 %copy-start.1 = (bf16[16,2,16,512]{3,2,1,0:T(8,128)(2,1)S(1)}, bf16[16,2,16,512]{3,2,1,0:T(8,128)(2,1)}, u32[]{:S(2)}) copy-start(bf16[16,2,16,512]{3,2,1,0:T(8,128)(2,1)} %param.7) | copy-start | bytes 1572868
  4.4 0.7 copy-start.3
  5.1 26.9 %copy-start.5 = (s32[32,1]{0,1:T(1,128)S(1)}, s32[32,1]{0,1:T(1,128)}, u32[]{:S(2)}) copy-start(s32[32,1]{0,1:T(1,128)} %param.11) | copy-start | bytes 388
  10.2 30.6 %copy-start.2 = (bf16[4,2,256,32]{2,3,1,0:T(8,128)(2,1)S(1)}, bf16[4,2,256,32]{2,3,1,0:T(8,128)(2,1)}, u32[]{:S(2)}) copy-start(bf16[4,2,256,32]{2,3,1,0:T(8,128)(2,1)} %param.13) | copy-start | bytes 393220
  31.2 9.5 %collective-permute-start = (bf16[64,2,4,512]{3,0,2,1:T(8,128)(2,1)S(1)}, bf16[64,2,4,512]{3,0,2,1:T(8,128)(2,1)S(1)}, u32[]{:S(2)}, u32[]{:S(2)}) collective-permute-start(bf16[64,2,4,512]{3,0,2,1:T(8,128)(2,1)S(1)} %bitcast.196), channel_id=1, source_target_pairs={{0,1},{1,2},{2,3},{3,0},{4,5},{5,6},{6,7},{7,4},{8,9},{9,10},{10,1... | collective-permute-start | bytes 1572872 | tf_op jit(solution)/shard_map/ppermute | solution.py:24
  34.1 11.1 %collective-permute-start.2 = (bf16[64,2,4,512]{3,0,2,1:T(8,128)(2,1)S(1)}, bf16[64,2,4,512]{3,0,2,1:T(8,128)(2,1)S(1)}, u32[]{:S(2)}, u32[]{:S(2)}) collective-permute-start(bf16[64,2,4,512]{3,0,2,1:T(8,128)(2,1)S(1)} %bitcast.197), channel_id=1, source_target_pairs={{1,0},{2,1},{3,2},{0,3},{5,4},{6,5},{7,6},{4,7},{9,8},{10,9},{11,1... | collective-permute-start | bytes 1572872 | tf_op jit(solution)/shard_map/ppermute | solution.py:26
  40.7 10.4 %collective-permute-start.1 = (bf16[64,2,4,512]{3,0,2,1:T(8,128)(2,1)S(1)}, bf16[64,2,4,512]{3,0,2,1:T(8,128)(2,1)S(1)}, u32[]{:S(2)}, u32[]{:S(2)}) collective-permute-start(bf16[64,2,4,512]{3,0,2,1:T(8,128)(2,1)S(1)} %collective-permute-done), channel_id=1, source_target_pairs={{0,1},{1,2},{2,3},{3,0},{4,5},{5,6},{6,7},{7,4},{8,9},{9,10},{10,1... | collective-permute-start | bytes 1572872 | tf_op jit(solution)/shard_map/ppermute | solution.py:24
  64.3 6.9 %copy-start.4 = (f32[16,16]{1,0:T(8,128)S(1)}, f32[16,16]{1,0:T(8,128)}, u32[]{:S(2)}) copy-start(f32[16,16]{1,0:T(8,128)} %param.9) | copy-start | bytes 3076
  67.4 51.3 %all-to-all-start.1 = ((bf16[256,2,4,512]{3,2,1,0:T(4,128)(2,1)}), bf16[256,2,4,512]{3,2,1,0:T(4,128)(2,1)S(1)}, u32[]{:S(2)}, u32[]{:S(2)}) async-start(bf16[256,2,4,512]{3,2,1,0:T(4,128)(2,1)} %copy.65), calls=%async_computation.1 | async-start | bytes 4194304 | tf_op jit(solution)/shard_map/all_to_all | solution.py:124
